TPU v7x, 32 devices: a whole 2x2x4 slice. The times are simulated.
32 devices in a mesh: site: 8 (over y, x, core), real: 4 (over z).
Axes of the slice: x: 2, y: 2, z: 4, core: 2. Of those that a mesh axis runs over, the one named last changes fastest.
Arguments:
- field: float32 [64, 16384], P('real', 'site'), may hold values from -6 to 6
- observed: float32 [20480], P('site'), may hold values from -6 to 6
- inv_cov: float32 [20480, 20480], P('site', 'real'), may hold values from -0.0012207031 to 0.0012207031
- site_xy: float32 [2, 16384], P(None, 'site'), may hold values from 0 to 200
- station_site: int32 [20480], P('site'), may hold values from 0 to 16383, as said below
- site_mean: float32 [16384], P('site'), may hold values from -3 to 0
- building_site: int32 [32768], P('site'), may hold values from 0 to 16383, as said below
- building_class: int32 [32768], P('site'), may hold values from 0 to 35
- building_tract: int32 [32768], P('site'), may hold values from 0 to 4095
- building_value: float32 [32768], P('site')
- median_ln: float32 [4, 36], replicated, may hold values from -2.3 to 0.4
- beta_ln: float32 [36], replicated, may hold values from 0.4 to 0.8
- loss_step: float32 [4, 36], replicated, may hold values from 0.02 to 0.3
Outputs:
- cond_field: float32 [64, 16384], P('real', 'site')
- tract_loss: float32 [64, 4096], P('real', 'site')
- total_loss: float32 [64], P('real')
Inputs may be any that keep to these rules, and one draw needn't show every extreme that they name: `station_site`: the stations of rows d * 2560 to (d + 1) * 2560 - 1 stand at sites d * 2048 to (d + 1) * 2048 - 1; several stations may share a site. `building_site`: the buildings of rows d * 4096 to (d + 1) * 4096 - 1 stand at sites d * 2048 to (d + 1) * 2048 - 1.
All inputs are finite; a program needn't handle non-finite values.
Results may differ from a plain program's by a relative error of at most 0.003.
Values may be sent and summed in bfloat16 or wider, within the bound.
A program may use at most 128 MiB of HBM per device.

v0:
```python
import math
import jax
import jax.numpy as jnp
from jax import lax
from jax.sharding import PartitionSpec as P

TRACT_DEV = 512


def normal_cdf(value):
    return 0.5 * (1.0 + lax.erf(value * 0.7071067811865476))


def shards(
    field,
    observed,
    inv_cov,
    site_xy,
    station_site,
    site_mean,
    building_site,
    building_class,
    building_tract,
    building_value,
    median_ln,
    beta_ln,
    loss_step,
):
    real_rows = field.shape[0]
    site_block = field.shape[1]
    site_count = lax.axis_size("site")
    first_site = lax.axis_index("site") * site_block
    station_local = station_site - first_site
    station_field = jnp.take(field, station_local, axis=1)
    innov = observed[None, :] - station_field
    partial_w = jnp.dot(
        lax.all_gather(innov, "real", axis=0, tiled=True),
        inv_cov,
        precision=lax.Precision.HIGHEST,
        preferred_element_type=jnp.float32,
    )
    station_xy = jnp.take(site_xy, station_local, axis=1)
    block_width = math.gcd(site_block, 256)
    summed = lax.psum(partial_w, "site")
    weights = lax.all_to_all(
        summed.astype(jnp.bfloat16), "real", split_axis=0, concat_axis=1, tiled=True
    )
    piece = lax.all_gather(station_xy, "site", axis=1, tiled=True)

    def one_block(index, acc):
        anchor = index * block_width
        east = lax.dynamic_slice_in_dim(site_xy[0], anchor, block_width)
        north = lax.dynamic_slice_in_dim(site_xy[1], anchor, block_width)
        dist = jnp.sqrt(
            (east[:, None] - piece[0][None, :]) ** 2 + (north[:, None] - piece[1][None, :]) ** 2
        )
        cross = jnp.exp(-dist / 30.0).astype(jnp.bfloat16)
        term = lax.dot_general(
            weights, cross, (((1,), (1,)), ((), ())), preferred_element_type=jnp.float32
        )
        current = lax.dynamic_slice_in_dim(acc, anchor, block_width, 1)
        return lax.dynamic_update_slice_in_dim(acc, current + term, anchor, 1)

    cond_field = lax.fori_loop(0, site_block // block_width, one_block, field)
    ln_im = site_mean[None, :] + 0.6 * cond_field
    build_local = building_site - first_site
    build_im = jnp.take(ln_im, build_local, axis=1)
    class_count = median_ln.shape[1]
    class_table = (
        building_class[:, None] == jnp.arange(class_count, dtype=jnp.int32)[None, :]
    ).astype(jnp.float32)
    median_b = jnp.dot(
        median_ln,
        class_table.T,
        precision=lax.Precision.HIGHEST,
        preferred_element_type=jnp.float32,
    )
    step_b = jnp.dot(
        loss_step,
        class_table.T,
        precision=lax.Precision.HIGHEST,
        preferred_element_type=jnp.float32,
    )
    beta_b = jnp.dot(
        beta_ln[None, :],
        class_table.T,
        precision=lax.Precision.HIGHEST,
        preferred_element_type=jnp.float32,
    )
    exceed = normal_cdf((build_im[None, :, :] - median_b[:, None, :]) / beta_b[:, None, :])
    loss = building_value[None, :] * jnp.sum(exceed * step_b[:, None, :], axis=0)
    build_count = loss.shape[1]
    tract_count = TRACT_DEV * site_count
    group_width = math.gcd(build_count, 512)
    groups = build_count // group_width
    loss_groups = loss.reshape(real_rows, groups, group_width).transpose(1, 0, 2)
    tract_groups = building_tract.reshape(groups, group_width)

    def add_group(acc, pair):
        loss_part, tracts = pair
        table = (tracts[:, None] == jnp.arange(tract_count, dtype=jnp.int32)[None, :]).astype(
            jnp.float32
        )
        return (
            acc
            + jnp.dot(
                loss_part,
                table,
                precision=lax.Precision.HIGHEST,
                preferred_element_type=jnp.float32,
            ),
            None,
        )

    tract_part, _ = lax.scan(
        add_group, jnp.zeros((real_rows, tract_count), jnp.float32), (loss_groups, tract_groups)
    )
    all_buildings = build_count * site_count
    tract_loss = lax.psum_scatter(tract_part, "site", scatter_dimension=1, tiled=True)
    total_loss = lax.psum(jnp.sum(tract_loss, axis=1), "site") / all_buildings
    return (cond_field, tract_loss, total_loss)


def solution(mesh):
    placed = (
        P("real", "site"),
        P("site"),
        P("site", "real"),
        P(None, "site"),
        P("site"),
        P("site"),
        P("site"),
        P("site"),
        P("site"),
        P("site"),
        P(),
        P(),
        P(),
    )
    return jax.shard_map(
        shards,
        mesh=mesh,
        in_specs=placed,
        out_specs=(P("real", "site"), P("real", "site"), P("real")),
        check_vma=False,
    )
```

profile of v0, /device:TPU:0, one launch (start us, length us, event | category | flops | bytes accessed | tf_op | source)
XLA Modules:
  0.0 375.5 jit_solution(16030790064351147388)
XLA Ops:
  7.2 0.0 copy-start
  7.2 0.0 copy-start.8
  7.2 0.9 copy.84
  8.1 0.7 compare_and_fusion.1
  8.8 0.3 copy.54
  9.2 4.2 %gather_fusion.1 = f32[2560,16]{1,0:T(8,128)S(1)} fusion(f32[16,2048]{0,1:T(8,128)S(1)} %copy.54, s32[3072]{0:T(1024)S(1)} %pad_clamp_fusion), kind=kCustom, calls=%fused_computation.1 | custom fusion | bytes 337920 | tf_op jit(solution)/shard_map/jit(_take)/gather | solution.py:34
  13.3 0.0 copy-done.8
  13.3 1.8 subtract_bitcast_fusion
  15.1 0.4 copy.55
  15.5 19.6 %all_gather.7 = f32[64,2560]{1,0:T(8,128)S(1)} all-gather(f32[16,2560]{1,0:T(8,128)S(1)} %copy.55), channel_id=1, replica_groups=mesh['site'=8,'real'=4] {'real'}, dimensions={0}, use_global_device_ids=true | all-gather | bytes 819200 | tf_op jit(solution)/shard_map/all_gather | solution.py:37
  35.1 36.5 %fusion.17 = f32[64,5120]{1,0:T(8,128)S(1)} fusion(f32[64,2560]{1,0:T(8,128)S(1)} %all_gather.7, f32[2560,5120]{1,0:T(8,128)} %param.19), kind=kOutput, calls=%fused_computation.42 | convolution fusion | flops 10066329600 | bytes 54394880 | tf_op jit(solution)/shard_map/dot_general | solution.py:36
  71.6 0.0 copy-start.3
  71.6 51.6 %all-reduce.1 = bf16[64,5120]{1,0:T(8,128)(2,1)} all-reduce(f32[64,5120]{1,0:T(8,128)S(1)} %fusion.17), channel_id=1, replica_groups=mesh['site'=8,'real'=4] {'site'}, use_global_device_ids=true, to_apply=%region_0.1 | all-reduce | flops 327680 | bytes 1966080 | tf_op jit(solution)/shard_map/psum | solution.py:44
  123.2 3.9 %all-to-all-start = ((bf16[4,16,5120]{2,1,0:T(8,128)(2,1)}), bf16[4,16,5120]{2,1,0:T(8,128)(2,1)S(1)}, u32[]{:S(2)}, u32[]{:S(2)}) async-start(bf16[4,16,5120]{2,1,0:T(8,128)(2,1)} %bitcast.7), calls=%async_computation | async-start | bytes 1310720 | tf_op jit(solution)/shard_map/all_to_all | solution.py:45
  127.2 0.4 copy.53
  127.5 4.2 %gather_fusion = f32[2560,2]{1,0:T(8,128)S(1)} fusion(f32[2,2048]{0,1:T(8,128)S(1)} %copy.53, s32[3072]{0:T(1024)S(1)} %pad_clamp_fusion), kind=kCustom, calls=%fused_computation | custom fusion | bytes 51200 | tf_op jit(solution)/shard_map/jit(_take)/gather | solution.py:42
  131.7 1.4 select_bitcast_fusion.1
  133.1 51.1 %all_gather.6 = f32[2,20480]{0,1:T(8,128)} all-gather(f32[2,2560]{0,1:T(8,128)S(1)} %select_bitcast_fusion.1), channel_id=1, replica_groups=mesh['site'=8,'real'=4] {'site'}, dimensions={1}, use_global_device_ids=true | all-gather | bytes 184320 | tf_op jit(solution)/shard_map/all_gather | solution.py:48
  184.2 6.0 %copy.57 = f32[2,20480]{1,0:T(2,128)S(1)} copy(f32[2,20480]{0,1:T(8,128)} %all_gather.6) | data formatting | bytes 327680 | tf_op jit(solution)/shard_map/while | solution.py:64
  190.3 0.3 fusion.9
  190.7 0.3 fusion.8
  191.0 0.3 convolution_bitcast_fusion
  191.3 0.0 all-to-all-done
  191.4 0.0 copy-start.9
  191.4 87.1 %while.24 = (s32[]{:T(128)}, f32[16,2048]{1,0:T(8,128)S(1)}, f32[2,2048]{1,0:T(2,128)S(1)}, f32[2,20480]{1,0:T(2,128)S(1)}, bf16[16,20480]{1,0:T(8,128)(2,1)S(1)...) while((s32[]{:T(128)}, f32[16,2048]{1,0:T(8,128)S(1)}, f32[2,2048]{1,0:T(2,128)S(1)}, ...), condition=%wide.region_2.3_spmd, body=%wide.region_1.2_spmd.sunk | while | flops 209719296 | bytes 1218715 | solution.py:64
  191.6 0.1 fusion.29
  191.8 10.7 %fusion.31 = f32[16,2048]{1,0:T(8,128)S(1)} fusion(f32[16,2048]{1,0:T(8,128)S(1)} %get-tuple-element.281, s32[]{:T(128)S(6)} %select_n.57, bf16[16,20480]{1,0:T(8,128)(2,1)S(1)} %get-tuple-element.293, f32[20480]{0:T(1024)S(1)} %bitcast.59, f32[256]{0:T(256)S(1)} %bitcast.64, f32[20480]{0:T(1024)S(1)} %bitcast.58, f32[256]{0:T(256)S(1)} %bitcast.65), kind=kOutput, calls=%fused_computation.7.clone.1 | convolution fusion | flops 209719296 | bytes 854020 | tf_op jit(solution)/shard_map/while/body/eval_jaxpr/dot_general | solution.py:58
  202.5 0.1 fusion.29
  202.6 10.7 %fusion.31 = f32[16,2048]{1,0:T(8,128)S(1)} fusion(f32[16,2048]{1,0:T(8,128)S(1)} %get-tuple-element.281, s32[]{:T(128)S(6)} %select_n.57, bf16[16,20480]{1,0:T(8,128)(2,1)S(1)} %get-tuple-element.293, f32[20480]{0:T(1024)S(1)} %bitcast.59, f32[256]{0:T(256)S(1)} %bitcast.64, f32[20480]{0:T(1024)S(1)} %bitcast.58, f32[256]{0:T(256)S(1)} %bitcast.65), kind=kOutput, calls=%fused_computation.7.clone.1 | convolution fusion | flops 209719296 | bytes 854020 | tf_op jit(solution)/shard_map/while/body/eval_jaxpr/dot_general | solution.py:58
  213.3 0.1 fusion.29
  213.5 10.7 %fusion.31 = f32[16,2048]{1,0:T(8,128)S(1)} fusion(f32[16,2048]{1,0:T(8,128)S(1)} %get-tuple-element.281, s32[]{:T(128)S(6)} %select_n.57, bf16[16,20480]{1,0:T(8,128)(2,1)S(1)} %get-tuple-element.293, f32[20480]{0:T(1024)S(1)} %bitcast.59, f32[256]{0:T(256)S(1)} %bitcast.64, f32[20480]{0:T(1024)S(1)} %bitcast.58, f32[256]{0:T(256)S(1)} %bitcast.65), kind=kOutput, calls=%fused_computation.7.clone.1 | convolution fusion | flops 209719296 | bytes 854020 | tf_op jit(solution)/shard_map/while/body/eval_jaxpr/dot_general | solution.py:58
  224.2 0.1 fusion.29
  224.4 10.7 %fusion.31 = f32[16,2048]{1,0:T(8,128)S(1)} fusion(f32[16,2048]{1,0:T(8,128)S(1)} %get-tuple-element.281, s32[]{:T(128)S(6)} %select_n.57, bf16[16,20480]{1,0:T(8,128)(2,1)S(1)} %get-tuple-element.293, f32[20480]{0:T(1024)S(1)} %bitcast.59, f32[256]{0:T(256)S(1)} %bitcast.64, f32[20480]{0:T(1024)S(1)} %bitcast.58, f32[256]{0:T(256)S(1)} %bitcast.65), kind=kOutput, calls=%fused_computation.7.clone.1 | convolution fusion | flops 209719296 | bytes 854020 | tf_op jit(solution)/shard_map/while/body/eval_jaxpr/dot_general | solution.py:58
  235.0 0.1 fusion.29
  235.2 10.7 %fusion.31 = f32[16,2048]{1,0:T(8,128)S(1)} fusion(f32[16,2048]{1,0:T(8,128)S(1)} %get-tuple-element.281, s32[]{:T(128)S(6)} %select_n.57, bf16[16,20480]{1,0:T(8,128)(2,1)S(1)} %get-tuple-element.293, f32[20480]{0:T(1024)S(1)} %bitcast.59, f32[256]{0:T(256)S(1)} %bitcast.64, f32[20480]{0:T(1024)S(1)} %bitcast.58, f32[256]{0:T(256)S(1)} %bitcast.65), kind=kOutput, calls=%fused_computation.7.clone.1 | convolution fusion | flops 209719296 | bytes 854020 | tf_op jit(solution)/shard_map/while/body/eval_jaxpr/dot_general | solution.py:58
  245.9 0.1 fusion.29
  246.1 10.7 %fusion.31 = f32[16,2048]{1,0:T(8,128)S(1)} fusion(f32[16,2048]{1,0:T(8,128)S(1)} %get-tuple-element.281, s32[]{:T(128)S(6)} %select_n.57, bf16[16,20480]{1,0:T(8,128)(2,1)S(1)} %get-tuple-element.293, f32[20480]{0:T(1024)S(1)} %bitcast.59, f32[256]{0:T(256)S(1)} %bitcast.64, f32[20480]{0:T(1024)S(1)} %bitcast.58, f32[256]{0:T(256)S(1)} %bitcast.65), kind=kOutput, calls=%fused_computation.7.clone.1 | convolution fusion | flops 209719296 | bytes 854020 | tf_op jit(solution)/shard_map/while/body/eval_jaxpr/dot_general | solution.py:58
  256.8 0.1 fusion.29
  257.0 10.7 %fusion.31 = f32[16,2048]{1,0:T(8,128)S(1)} fusion(f32[16,2048]{1,0:T(8,128)S(1)} %get-tuple-element.281, s32[]{:T(128)S(6)} %select_n.57, bf16[16,20480]{1,0:T(8,128)(2,1)S(1)} %get-tuple-element.293, f32[20480]{0:T(1024)S(1)} %bitcast.59, f32[256]{0:T(256)S(1)} %bitcast.64, f32[20480]{0:T(1024)S(1)} %bitcast.58, f32[256]{0:T(256)S(1)} %bitcast.65), kind=kOutput, calls=%fused_computation.7.clone.1 | convolution fusion | flops 209719296 | bytes 854020 | tf_op jit(solution)/shard_map/while/body/eval_jaxpr/dot_general | solution.py:58
  267.6 0.1 fusion.29
  267.8 10.7 %fusion.31 = f32[16,2048]{1,0:T(8,128)S(1)} fusion(f32[16,2048]{1,0:T(8,128)S(1)} %get-tuple-element.281, s32[]{:T(128)S(6)} %select_n.57, bf16[16,20480]{1,0:T(8,128)(2,1)S(1)} %get-tuple-element.293, f32[20480]{0:T(1024)S(1)} %bitcast.59, f32[256]{0:T(256)S(1)} %bitcast.64, f32[20480]{0:T(1024)S(1)} %bitcast.58, f32[256]{0:T(256)S(1)} %bitcast.65), kind=kOutput, calls=%fused_computation.7.clone.1 | convolution fusion | flops 209719296 | bytes 854020 | tf_op jit(solution)/shard_map/while/body/eval_jaxpr/dot_general | solution.py:58
  278.5 0.0 copy-done.9
  278.5 0.3 copy.58
  278.9 14.1 %gather_fusion.2 = f32[4096,16]{1,0:T(8,128)} fusion(f32[16,2048]{0,1:T(8,128)S(1)} %copy.58, s32[4096]{0:T(1024)S(1)} %fusion.13), kind=kCustom, calls=%fused_computation.2 | custom fusion | bytes 540672 | tf_op jit(solution)/shard_map/jit(_take)/gather | solution.py:67
  293.0 3.6 select_bitcast_fusion
  296.6 0.6 copy.59
  297.2 0.3 multiply_reduce_fusion
  297.4 0.2 copy.63
  297.6 22.7 %while.25 = (s32[]{:T(128)}, f32[16,4096]{1,0:T(8,128)S(1)}, f32[8,16,512]{2,0,1:T(8,128)S(1)}, s32[8,512]{1,0:T(8,128)S(1)}, s32[]{:T(128)}, /*index=5*/s32[]{:T(128)}) while((s32[]{:T(128)}, f32[16,4096]{1,0:T(8,128)S(1)}, f32[8,16,512]{2,0,1:T(8,128)S(1)}, s32[8,512]{1,0:T(8,128)S(1)}, s32[]{:T(128)}, /*index=5*/s32[]{:T(128)}) %tuple.76), condition=%wide.region_5.6_spmd.clone, body=%wide.region_4.5_spmd.clone.sunk | while | flops 404881408 | bytes 628831 | solution.py:115
  297.7 2.8 fusion.32
  300.5 2.8 fusion.32
  303.4 2.8 fusion.32
  306.2 2.8 fusion.32
  309.1 2.8 fusion.32
  311.9 2.8 fusion.32
  314.7 2.8 fusion.32
  317.6 2.8 fusion.32
  320.3 0.0 copy-start.1
  320.4 0.7 copy-done.4
  321.0 0.0 reduce-scatter.2.cloned.1.call-update
  321.1 34.0 %reduce-scatter.2.cloned.1.call-done = f32[16,512]{1,0:T(8,128)} async-done(((f32[16,4096]{1,0:T(8,128)}), f32[16,512]{1,0:T(8,128)}) %reduce-scatter.2.cloned.1.call-update) | async-done | bytes 32784 | tf_op jit(solution)/shard_map/reduce_scatter | solution.py:119
  355.1 0.9 reduce_sum.22
  356.0 12.2 %psum.15 = f32[16]{0:T(128)S(1)} all-reduce(f32[16]{0:T(128)S(1)} %reduce_sum.22), channel_id=1, replica_groups=mesh['site'=8,'real'=4] {'site'}, use_global_device_ids=true, to_apply=%region_8.9 | all-reduce | flops 16 | bytes 128 | tf_op jit(solution)/shard_map/psum | solution.py:120
  368.2 0.5 broadcast_multiply_fusion
  (60 shorter events, 0.6 us)
Async XLA Ops:
  7.2 183.5 %copy-start = (f32[4,36]{1,0:T(4,128)S(1)}, f32[4,36]{1,0:T(4,128)}, u32[]{:S(2)}) copy-start(f32[4,36]{1,0:T(4,128)} %param.29) | copy-start | bytes 1732
  7.2 6.1 %copy-start.8 = (f32[2560]{0:T(1024)S(1)}, f32[2560]{0:T(1024)}, u32[]{:S(2)}) copy-start(f32[2560]{0:T(1024)} %param.18) | copy-start | bytes 30724
  71.6 55.6 %copy-start.3 = (f32[2,2048]{1,0:T(2,128)S(1)}, f32[2,2048]{1,0:T(2,128)}, u32[]{:S(2)}) copy-start(f32[2,2048]{1,0:T(2,128)} %param.20) | copy-start | bytes 49156
  123.2 68.1 %all-to-all-start = ((bf16[4,16,5120]{2,1,0:T(8,128)(2,1)}), bf16[4,16,5120]{2,1,0:T(8,128)(2,1)S(1)}, u32[]{:S(2)}, u32[]{:S(2)}) async-start(bf16[4,16,5120]{2,1,0:T(8,128)(2,1)} %bitcast.7), calls=%async_computation | async-start | bytes 1310720 | tf_op jit(solution)/shard_map/all_to_all | solution.py:45
  127.2 5.9 %copy-start.5 = (s32[4096]{0:T(1024)S(1)}, s32[4096]{0:T(1024)}, u32[]{:S(2)}) copy-start(s32[4096]{0:T(1024)} %param.23) | copy-start | bytes 49156
  127.2 227.9 %reduce-scatter.2.cloned.1.call-start = ((), (), s32[]{:S(2)}) async-start(), calls=%async_computation.2 | async-start | bytes 294912 | tf_op jit(solution)/shard_map/reduce_scatter | solution.py:119
  184.2 6.1 %copy-start.6 = (f32[4096]{0:T(1024)S(1)}, f32[4096]{0:T(1024)}, u32[]{:S(2)}) copy-start(f32[4096]{0:T(1024)} %param.26) | copy-start | bytes 49156
  184.2 6.1 %copy-start.7 = (s32[4096]{0:T(1024)S(1)}, s32[4096]{0:T(1024)}, u32[]{:S(2)}) copy-start(s32[4096]{0:T(1024)} %param.25) | copy-start | bytes 49156
  184.2 6.1 %copy-start.10 = (s32[4096]{0:T(1024)S(1)}, s32[4096]{0:T(1024)}, u32[]{:S(2)}) copy-start(s32[4096]{0:T(1024)} %param.24) | copy-start | bytes 49156
  184.2 6.1 %copy-start.12 = (f32[36]{0:T(128)S(1)}, f32[36]{0:T(128)}, u32[]{:S(2)}) copy-start(f32[36]{0:T(128)} %param.28) | copy-start | bytes 436
  184.2 6.8 %copy-start.11 = (f32[4,36]{1,0:T(4,128)S(1)}, f32[4,36]{1,0:T(4,128)}, u32[]{:S(2)}) copy-start(f32[4,36]{1,0:T(4,128)} %param.27) | copy-start | bytes 1732
  191.4 87.1 %copy-start.9 = (f32[2048]{0:T(1024)S(1)}, f32[2048]{0:T(1024)}, u32[]{:S(2)}) copy-start(f32[2048]{0:T(1024)} %param.22) | copy-start | bytes 24580
  278.5 18.1 %copy-start.2 = (f32[16,2048]{1,0:T(8,128)}, f32[16,2048]{1,0:T(8,128)S(1)}, u32[]{:S(2)}) copy-start(f32[16,2048]{1,0:T(8,128)S(1)} %get-tuple-element.116) | copy-start | bytes 393220
  320.3 0.7 copy-start.4
  320.3 48.4 %copy-start.1 = (f32[4,36]{1,0:T(4,128)S(1)}, f32[4,36]{1,0:T(4,128)}, u32[]{:S(2)}) copy-start(f32[4,36]{1,0:T(4,128)} %param.29) | copy-start | bytes 1732
Sparse Core Ops, SparseCore 0:
  321.2 33.8 reduce-scatter.1
where the time goes:
time: 376 us
  matrix products  145 us (39%)
  blocking collectives  135 us (36%)
  waiting for transfers between devices  34 us (9%)
  local copies, waits for them, and re-layouts  33.8 us (9%)
  between operations  14.3 us (4%)
  other arithmetic  9.19 us (2%)
  starting transfers between devices  3.94 us (1%)
    dot_general x8, matrix products, one_block(): lax.dot_general(weights, cross, (((1,), (1,)), ((), ())), preferred_eleme...  85.4 us
    psum x1, blocking collectives, shards(): summed = lax.psum(partial_w, 'site')  51.6 us
    all_gather x1, blocking collectives, shards(): piece = lax.all_gather(station_xy, 'site', axis=1, tiled=True)  51.1 us
    dot_general x1, matrix products, shards(): jnp.dot(lax.all_gather(innov, 'real', axis=0, tiled=True), inv_cov, preci...  36.5 us
    reduce_scatter x1, waiting for transfers between devices, shards(): lax.psum_scatter(tract_part, 'site', scatter_dimension=1, tiled=True)  34 us
    dot_general x8, matrix products, add_group(): jnp.dot(loss_part, table, precision=lax.Precision.HIGHEST, preferred_elem...  22.2 us
    all_gather x1, blocking collectives, shards(): lax.all_gather(innov, 'real', axis=0, tiled=True)  19.6 us
    gather x1, local copies, waits for them, and re-layouts, shards(): build_im = jnp.take(ln_im, build_local, axis=1)  14.1 us
  transfers between devices with their start and end apart: 2, of which 1 were waited for; matrix products, arithmetic and copies ran while one was open for 3% of the time, Pallas kernels for 0%

commit v1 on v0

--- a/solution.py
+++ b/solution.py
@@ -45,7 +45,12 @@
     weights = lax.all_to_all(
         summed.astype(jnp.bfloat16), "real", split_axis=0, concat_axis=1, tiled=True
     )
-    piece = lax.all_gather(station_xy, "site", axis=1, tiled=True)
+    ring = [station_xy]
+    for hop in range(7):
+        ring.append(lax.ppermute(ring[-1], "site", [(dev, (dev + 1) % 8) for dev in range(8)]))
+    piece = jnp.roll(
+        jnp.concatenate(ring[::-1], axis=1), (lax.axis_index("site") + 1) * ring[0].shape[1], axis=1
+    )
 
     def one_block(index, acc):
         anchor = index * block_width

time: 376 us -> 340 us (0.904)
  blocking collectives: 135 us -> 83.4 us
  waiting for transfers between devices: 34 us -> 53.2 us
  local copies, waits for them, and re-layouts: 33.8 us -> 29.4 us
    all_gather x1 -> x0, blocking collectives: 51.1 us -> none  [shards(): piece = lax.all_gather(station_xy, 'site', axis=1, tiled=True)]
    ppermute x0 -> x7, waiting for transfers between devices: none -> 19.4 us  [shards(): lax.ppermute(ring[-1], 'site', [(dev, (dev + 1) % 8) for dev in range(8)])]
    while x1 -> x0, local copies, waits for them, and re-layouts: 6.04 us -> none  [shards(): cond_field = lax.fori_loop(0, site_block // block_width, one_block, field)]
  transfers between devices with their start and end apart: 2 -> 9, of which waited for: 1 -> 6; matrix products, arithmetic and copies ran while one was open for 3% -> 13% of each run, Pallas kernels for 0% -> 0%
where the time goes in v1:
time: 340 us
  matrix products  145 us (43%)
  blocking collectives  83.4 us (25%)
  waiting for transfers between devices  53.2 us (16%)
  local copies, waits for them, and re-layouts  29.4 us (9%)
  between operations  14.4 us (4%)
  other arithmetic  9.19 us (3%)
  starting transfers between devices  4.68 us (1%)
    dot_general x8, matrix products, one_block(): lax.dot_general(weights, cross, (((1,), (1,)), ((), ())), preferred_eleme...  85.4 us
    psum x1, blocking collectives, shards(): summed = lax.psum(partial_w, 'site')  52.1 us
    dot_general x1, matrix products, shards(): jnp.dot(lax.all_gather(innov, 'real', axis=0, tiled=True), inv_cov, preci...  36.4 us
    reduce_scatter x1, waiting for transfers between devices, shards(): lax.psum_scatter(tract_part, 'site', scatter_dimension=1, tiled=True)  33.8 us
    dot_general x8, matrix products, add_group(): jnp.dot(loss_part, table, precision=lax.Precision.HIGHEST, preferred_elem...  22.2 us
    ppermute x7, waiting for transfers between devices, shards(): lax.ppermute(ring[-1], 'site', [(dev, (dev + 1) % 8) for dev in range(8)])  19.4 us
    all_gather x1, blocking collectives, shards(): lax.all_gather(innov, 'real', axis=0, tiled=True)  19.1 us
    gather x1, local copies, waits for them, and re-layouts, shards(): build_im = jnp.take(ln_im, build_local, axis=1)  14.2 us
  transfers between devices with their start and end apart: 9, of which 6 were waited for; matrix products, arithmetic and copies ran while one was open for 13% of the time, Pallas kernels for 0%

profile of v1, /device:TPU:0, one launch (start us, length us, event | category | flops | bytes accessed | tf_op | source)
XLA Modules:
  0.0 339.9 jit_solution(6694586034641494480)
XLA Ops:
  7.2 0.9 copy.105
  8.1 0.7 compare_and_fusion.1
  8.8 1.1 copy.57
  9.9 4.1 %gather_fusion = f32[2560,2]{1,0:T(8,128)S(1)} fusion(f32[2,2048]{0,1:T(8,128)S(1)} %copy.57, s32[3072]{0:T(1024)S(1)} %pad_clamp_fusion), kind=kCustom, calls=%fused_computation | custom fusion | bytes 51200 | tf_op jit(solution)/shard_map/jit(_take)/gather | solution.py:42
  14.1 1.4 select_bitcast_fusion.1
  15.4 0.4 copy.58
  15.8 0.5 collective-permute-start
  16.3 0.3 copy.61
  16.6 4.1 %gather_fusion.1 = f32[2560,16]{1,0:T(8,128)S(1)} fusion(f32[16,2048]{0,1:T(8,128)S(1)} %copy.61, s32[3072]{0:T(1024)S(1)} %pad_clamp_fusion), kind=kCustom, calls=%fused_computation.1 | custom fusion | bytes 337920 | tf_op jit(solution)/shard_map/jit(_take)/gather | solution.py:34
  20.8 1.8 subtract_bitcast_fusion
  22.6 0.4 copy.62
  23.0 19.1 %all_gather.3 = f32[64,2560]{1,0:T(8,128)S(1)} all-gather(f32[16,2560]{1,0:T(8,128)S(1)} %copy.62), channel_id=1, replica_groups=mesh['site'=8,'real'=4] {'real'}, dimensions={0}, use_global_device_ids=true | all-gather | bytes 819200 | tf_op jit(solution)/shard_map/all_gather | solution.py:37
  42.0 36.4 %fusion.17 = f32[64,5120]{1,0:T(8,128)S(1)} fusion(f32[64,2560]{1,0:T(8,128)S(1)} %all_gather.3, f32[2560,5120]{1,0:T(8,128)} %param.19), kind=kOutput, calls=%fused_computation.59 | convolution fusion | flops 10066329600 | bytes 54394880 | tf_op jit(solution)/shard_map/dot_general | solution.py:36
  78.6 0.2 collective-permute-start.1
  78.7 52.1 %all-reduce.1 = bf16[64,5120]{1,0:T(8,128)(2,1)} all-reduce(f32[64,5120]{1,0:T(8,128)S(1)} %fusion.17), channel_id=1, replica_groups=mesh['site'=8,'real'=4] {'site'}, use_global_device_ids=true, to_apply=%region_0.1 | all-reduce | flops 327680 | bytes 1966080 | tf_op jit(solution)/shard_map/psum | solution.py:44
  130.9 4.0 %all-to-all-start = ((bf16[4,16,5120]{2,1,0:T(8,128)(2,1)}), bf16[4,16,5120]{2,1,0:T(8,128)(2,1)S(1)}, u32[]{:S(2)}, u32[]{:S(2)}) async-start(bf16[4,16,5120]{2,1,0:T(8,128)(2,1)} %bitcast.7), calls=%async_computation | async-start | bytes 1310720 | tf_op jit(solution)/shard_map/all_to_all | solution.py:45
  134.8 0.1 collective-permute-start.2
  134.9 0.3 convolution_bitcast_fusion
  135.2 3.7 %collective-permute-done.2 = f32[2,2560]{1,0:T(2,128)S(1)} collective-permute-done((f32[2,2560]{1,0:T(2,128)S(1)}, f32[2,2560]{1,0:T(2,128)S(1)}, u32[]{:S(2)}, u32[]{:S(2)}) %collective-permute-start.2) | collective-permute-done | bytes 20512 | tf_op jit(solution)/shard_map/ppermute | solution.py:50
  139.0 0.3 fusion.8
  139.3 3.8 %collective-permute-done.3 = f32[2,2560]{1,0:T(2,128)S(1)} collective-permute-done((f32[2,2560]{1,0:T(2,128)S(1)}, f32[2,2560]{1,0:T(2,128)S(1)}, u32[]{:S(2)}, u32[]{:S(2)}) %collective-permute-start.3) | collective-permute-done | bytes 20512 | tf_op jit(solution)/shard_map/ppermute | solution.py:50
  143.1 0.3 fusion.9
  143.4 3.8 %collective-permute-done.4 = f32[2,2560]{1,0:T(2,128)S(1)} collective-permute-done((f32[2,2560]{1,0:T(2,128)S(1)}, f32[2,2560]{1,0:T(2,128)S(1)}, u32[]{:S(2)}, u32[]{:S(2)}) %collective-permute-start.4) | collective-permute-done | bytes 20512 | tf_op jit(solution)/shard_map/ppermute | solution.py:50
  147.2 4.1 %collective-permute-done.5 = f32[2,2560]{1,0:T(2,128)S(1)} collective-permute-done((f32[2,2560]{1,0:T(2,128)S(1)}, f32[2,2560]{1,0:T(2,128)S(1)}, u32[]{:S(2)}, u32[]{:S(2)}) %collective-permute-start.5) | collective-permute-done | bytes 20512 | tf_op jit(solution)/shard_map/ppermute | solution.py:50
  151.4 4.0 %collective-permute-done.6 = f32[2,2560]{1,0:T(2,128)S(1)} collective-permute-done((f32[2,2560]{1,0:T(2,128)S(1)}, f32[2,2560]{1,0:T(2,128)S(1)}, u32[]{:S(2)}, u32[]{:S(2)}) %collective-permute-start.6) | collective-permute-done | bytes 20512 | tf_op jit(solution)/shard_map/ppermute | solution.py:50
  155.6 0.2 constant_dynamic-slice_fusion.4
  156.0 87.1 %while.24 = (s32[]{:T(128)}, f32[16,2048]{1,0:T(8,128)S(1)}, f32[2,2048]{1,0:T(2,128)S(1)}, f32[2,20480]{1,0:T(2,128)S(1)}, bf16[16,20480]{1,0:T(8,128)(2,1)S(1)...) while((s32[]{:T(128)}, f32[16,2048]{1,0:T(8,128)S(1)}, f32[2,2048]{1,0:T(2,128)S(1)}, ...), condition=%wide.region_2.3_spmd, body=%wide.region_1.2_spmd.sunk | while | flops 209719296 | bytes 1218707 | solution.py:69
  156.2 0.1 fusion.29
  156.3 10.7 %fusion.31 = f32[16,2048]{1,0:T(8,128)S(1)} fusion(f32[16,2048]{1,0:T(8,128)S(1)} %get-tuple-element.266, s32[]{:T(128)S(6)} %select_n.72, bf16[16,20480]{1,0:T(8,128)(2,1)S(1)} %get-tuple-element.278, f32[20480]{0:T(1024)S(1)} %bitcast.59, f32[256]{0:T(256)S(1)} %bitcast.64, f32[20480]{0:T(1024)S(1)} %bitcast.58, f32[256]{0:T(256)S(1)} %bitcast.65), kind=kOutput, calls=%fused_computation.7.clone.1 | convolution fusion | flops 209719296 | bytes 854020 | tf_op jit(solution)/shard_map/while/body/eval_jaxpr/dot_general | solution.py:63
  167.1 0.1 fusion.29
  167.2 10.7 %fusion.31 = f32[16,2048]{1,0:T(8,128)S(1)} fusion(f32[16,2048]{1,0:T(8,128)S(1)} %get-tuple-element.266, s32[]{:T(128)S(6)} %select_n.72, bf16[16,20480]{1,0:T(8,128)(2,1)S(1)} %get-tuple-element.278, f32[20480]{0:T(1024)S(1)} %bitcast.59, f32[256]{0:T(256)S(1)} %bitcast.64, f32[20480]{0:T(1024)S(1)} %bitcast.58, f32[256]{0:T(256)S(1)} %bitcast.65), kind=kOutput, calls=%fused_computation.7.clone.1 | convolution fusion | flops 209719296 | bytes 854020 | tf_op jit(solution)/shard_map/while/body/eval_jaxpr/dot_general | solution.py:63
  177.9 0.1 fusion.29
  178.1 10.7 %fusion.31 = f32[16,2048]{1,0:T(8,128)S(1)} fusion(f32[16,2048]{1,0:T(8,128)S(1)} %get-tuple-element.266, s32[]{:T(128)S(6)} %select_n.72, bf16[16,20480]{1,0:T(8,128)(2,1)S(1)} %get-tuple-element.278, f32[20480]{0:T(1024)S(1)} %bitcast.59, f32[256]{0:T(256)S(1)} %bitcast.64, f32[20480]{0:T(1024)S(1)} %bitcast.58, f32[256]{0:T(256)S(1)} %bitcast.65), kind=kOutput, calls=%fused_computation.7.clone.1 | convolution fusion | flops 209719296 | bytes 854020 | tf_op jit(solution)/shard_map/while/body/eval_jaxpr/dot_general | solution.py:63
  188.8 0.1 fusion.29
  188.9 10.7 %fusion.31 = f32[16,2048]{1,0:T(8,128)S(1)} fusion(f32[16,2048]{1,0:T(8,128)S(1)} %get-tuple-element.266, s32[]{:T(128)S(6)} %select_n.72, bf16[16,20480]{1,0:T(8,128)(2,1)S(1)} %get-tuple-element.278, f32[20480]{0:T(1024)S(1)} %bitcast.59, f32[256]{0:T(256)S(1)} %bitcast.64, f32[20480]{0:T(1024)S(1)} %bitcast.58, f32[256]{0:T(256)S(1)} %bitcast.65), kind=kOutput, calls=%fused_computation.7.clone.1 | convolution fusion | flops 209719296 | bytes 854020 | tf_op jit(solution)/shard_map/while/body/eval_jaxpr/dot_general | solution.py:63
  199.6 0.1 fusion.29
  199.8 10.7 %fusion.31 = f32[16,2048]{1,0:T(8,128)S(1)} fusion(f32[16,2048]{1,0:T(8,128)S(1)} %get-tuple-element.266, s32[]{:T(128)S(6)} %select_n.72, bf16[16,20480]{1,0:T(8,128)(2,1)S(1)} %get-tuple-element.278, f32[20480]{0:T(1024)S(1)} %bitcast.59, f32[256]{0:T(256)S(1)} %bitcast.64, f32[20480]{0:T(1024)S(1)} %bitcast.58, f32[256]{0:T(256)S(1)} %bitcast.65), kind=kOutput, calls=%fused_computation.7.clone.1 | convolution fusion | flops 209719296 | bytes 854020 | tf_op jit(solution)/shard_map/while/body/eval_jaxpr/dot_general | solution.py:63
  210.5 0.1 fusion.29
  210.6 10.7 %fusion.31 = f32[16,2048]{1,0:T(8,128)S(1)} fusion(f32[16,2048]{1,0:T(8,128)S(1)} %get-tuple-element.266, s32[]{:T(128)S(6)} %select_n.72, bf16[16,20480]{1,0:T(8,128)(2,1)S(1)} %get-tuple-element.278, f32[20480]{0:T(1024)S(1)} %bitcast.59, f32[256]{0:T(256)S(1)} %bitcast.64, f32[20480]{0:T(1024)S(1)} %bitcast.58, f32[256]{0:T(256)S(1)} %bitcast.65), kind=kOutput, calls=%fused_computation.7.clone.1 | convolution fusion | flops 209719296 | bytes 854020 | tf_op jit(solution)/shard_map/while/body/eval_jaxpr/dot_general | solution.py:63
  221.4 0.1 fusion.29
  221.5 10.7 %fusion.31 = f32[16,2048]{1,0:T(8,128)S(1)} fusion(f32[16,2048]{1,0:T(8,128)S(1)} %get-tuple-element.266, s32[]{:T(128)S(6)} %select_n.72, bf16[16,20480]{1,0:T(8,128)(2,1)S(1)} %get-tuple-element.278, f32[20480]{0:T(1024)S(1)} %bitcast.59, f32[256]{0:T(256)S(1)} %bitcast.64, f32[20480]{0:T(1024)S(1)} %bitcast.58, f32[256]{0:T(256)S(1)} %bitcast.65), kind=kOutput, calls=%fused_computation.7.clone.1 | convolution fusion | flops 209719296 | bytes 854020 | tf_op jit(solution)/shard_map/while/body/eval_jaxpr/dot_general | solution.py:63
  232.2 0.1 fusion.29
  232.4 10.7 %fusion.31 = f32[16,2048]{1,0:T(8,128)S(1)} fusion(f32[16,2048]{1,0:T(8,128)S(1)} %get-tuple-element.266, s32[]{:T(128)S(6)} %select_n.72, bf16[16,20480]{1,0:T(8,128)(2,1)S(1)} %get-tuple-element.278, f32[20480]{0:T(1024)S(1)} %bitcast.59, f32[256]{0:T(256)S(1)} %bitcast.64, f32[20480]{0:T(1024)S(1)} %bitcast.58, f32[256]{0:T(256)S(1)} %bitcast.65), kind=kOutput, calls=%fused_computation.7.clone.1 | convolution fusion | flops 209719296 | bytes 854020 | tf_op jit(solution)/shard_map/while/body/eval_jaxpr/dot_general | solution.py:63
  243.1 0.3 copy.64
  243.4 14.2 %gather_fusion.2 = f32[4096,16]{1,0:T(8,128)} fusion(f32[16,2048]{0,1:T(8,128)S(1)} %copy.64, s32[4096]{0:T(1024)S(1)} %fusion.13), kind=kCustom, calls=%fused_computation.2 | custom fusion | bytes 540672 | tf_op jit(solution)/shard_map/jit(_take)/gather | solution.py:72
  257.6 3.6 %select_bitcast_fusion = f32[16,4096]{0,1:T(8,128)S(1)} fusion(f32[4096,16]{1,0:T(8,128)} %gather_fusion.2, pred[4096]{0:T(1024)(128)(4,1)S(1)} %compare_and_fusion), kind=kLoop, calls=%fused_computation.21 | loop fusion | flops 65536 | bytes 528384 | tf_op jit(solution)/shard_map/jit(_take)/select_n | solution.py:72
  261.2 0.6 copy.65
  261.8 0.3 multiply_reduce_fusion
  262.1 0.2 copy.69
  262.3 22.7 %while.25 = (s32[]{:T(128)}, f32[16,4096]{1,0:T(8,128)S(1)}, f32[8,16,512]{2,0,1:T(8,128)S(1)}, s32[8,512]{1,0:T(8,128)S(1)}, s32[]{:T(128)}, /*index=5*/s32[]{:T(128)}) while((s32[]{:T(128)}, f32[16,4096]{1,0:T(8,128)S(1)}, f32[8,16,512]{2,0,1:T(8,128)S(1)}, s32[8,512]{1,0:T(8,128)S(1)}, s32[]{:T(128)}, /*index=5*/s32[]{:T(128)}) %tuple.73), condition=%wide.region_5.6_spmd.clone, body=%wide.region_4.5_spmd.clone.sunk | while | flops 404881408 | bytes 628823 | solution.py:120
  262.3 2.8 fusion.32
  265.2 2.8 fusion.32
  268.0 2.8 fusion.32
  270.9 2.8 fusion.32
  273.7 2.8 fusion.32
  276.5 2.8 fusion.32
  279.4 2.8 fusion.32
  282.2 2.8 fusion.32
  285.0 0.7 copy-done.4
  285.7 0.0 reduce-scatter.2.cloned.1.call-update
  285.7 33.8 %reduce-scatter.2.cloned.1.call-done = f32[16,512]{1,0:T(8,128)} async-done(((f32[16,4096]{1,0:T(8,128)}), f32[16,512]{1,0:T(8,128)}) %reduce-scatter.2.cloned.1.call-update) | async-done | bytes 32784 | tf_op jit(solution)/shard_map/reduce_scatter | solution.py:124
  319.5 0.9 reduce_sum.22
  320.4 12.2 %psum.15 = f32[16]{0:T(128)S(1)} all-reduce(f32[16]{0:T(128)S(1)} %reduce_sum.22), channel_id=1, replica_groups=mesh['site'=8,'real'=4] {'site'}, use_global_device_ids=true, to_apply=%region_8.9 | all-reduce | flops 16 | bytes 128 | tf_op jit(solution)/shard_map/psum | solution.py:125
  332.6 0.5 broadcast_multiply_fusion
  (90 shorter events, 0.9 us)
Async XLA Ops:
  7.2 127.7 %copy-start = (f32[4,36]{1,0:T(4,128)S(1)}, f32[4,36]{1,0:T(4,128)}, u32[]{:S(2)}) copy-start(f32[4,36]{1,0:T(4,128)} %param.27) | copy-start | bytes 1732
  15.4 5.4 %copy-start.8 = (f32[2560]{0:T(1024)S(1)}, f32[2560]{0:T(1024)}, u32[]{:S(2)}) copy-start(f32[2560]{0:T(1024)} %param.18) | copy-start | bytes 30724
  15.8 62.7 %collective-permute-start = (f32[2,2560]{1,0:T(2,128)S(1)}, f32[2,2560]{1,0:T(2,128)S(1)}, u32[]{:S(2)}, u32[]{:S(2)}) collective-permute-start(f32[2,2560]{1,0:T(2,128)S(1)} %copy.58), channel_id=1, source_target_pairs={{0,4},{4,8},{8,12},{12,16},{16,20},{20,24},{24,28},{28,0},{1,5},{5... | collective-permute-start | bytes 61448 | tf_op jit(solution)/shard_map/ppermute | solution.py:50
  78.5 56.4 %copy-start.10 = (s32[4096]{0:T(1024)S(1)}, s32[4096]{0:T(1024)}, u32[]{:S(2)}) copy-start(s32[4096]{0:T(1024)} %param.24) | copy-start | bytes 49156
  78.5 60.5 %copy-start.11 = (f32[4,36]{1,0:T(4,128)S(1)}, f32[4,36]{1,0:T(4,128)}, u32[]{:S(2)}) copy-start(f32[4,36]{1,0:T(4,128)} %param.29) | copy-start | bytes 1732
  78.5 64.6 %copy-start.12 = (f32[36]{0:T(128)S(1)}, f32[36]{0:T(128)}, u32[]{:S(2)}) copy-start(f32[36]{0:T(128)} %param.28) | copy-start | bytes 436
  78.5 68.7 %copy-start.5 = (s32[4096]{0:T(1024)S(1)}, s32[4096]{0:T(1024)}, u32[]{:S(2)}) copy-start(s32[4096]{0:T(1024)} %param.23) | copy-start | bytes 49156
  78.5 72.8 %copy-start.6 = (f32[4096]{0:T(1024)S(1)}, f32[4096]{0:T(1024)}, u32[]{:S(2)}) copy-start(f32[4096]{0:T(1024)} %param.26) | copy-start | bytes 49156
  78.5 72.8 %copy-start.7 = (s32[4096]{0:T(1024)S(1)}, s32[4096]{0:T(1024)}, u32[]{:S(2)}) copy-start(s32[4096]{0:T(1024)} %param.25) | copy-start | bytes 49156
  78.6 56.3 %collective-permute-start.1 = (f32[2,2560]{1,0:T(2,128)S(1)}, f32[2,2560]{1,0:T(2,128)S(1)}, u32[]{:S(2)}, u32[]{:S(2)}) collective-permute-start(f32[2,2560]{1,0:T(2,128)S(1)} %collective-permute-done), channel_id=1, source_target_pairs={{0,4},{4,8},{8,12},{12,16},{16,20},{20,24},{24,28},{28,0},{1,5},{5... | collective-permute-start | bytes 61448 | tf_op jit(solution)/shard_map/ppermute | solution.py:50
  130.8 25.1 %copy-start.3 = (f32[2,2048]{1,0:T(2,128)S(1)}, f32[2,2048]{1,0:T(2,128)}, u32[]{:S(2)}) copy-start(f32[2,2048]{1,0:T(2,128)} %param.20) | copy-start | bytes 49156
  130.9 25.0 %all-to-all-start = ((bf16[4,16,5120]{2,1,0:T(8,128)(2,1)}), bf16[4,16,5120]{2,1,0:T(8,128)(2,1)S(1)}, u32[]{:S(2)}, u32[]{:S(2)}) async-start(bf16[4,16,5120]{2,1,0:T(8,128)(2,1)} %bitcast.7), calls=%async_computation | async-start | bytes 1310720 | tf_op jit(solution)/shard_map/all_to_all | solution.py:45
  134.8 184.7 %reduce-scatter.2.cloned.1.call-start = ((), (), s32[]{:S(2)}) async-start(), calls=%async_computation.2 | async-start | bytes 294912 | tf_op jit(solution)/shard_map/reduce_scatter | solution.py:124
  134.8 4.2 %collective-permute-start.2 = (f32[2,2560]{1,0:T(2,128)S(1)}, f32[2,2560]{1,0:T(2,128)S(1)}, u32[]{:S(2)}, u32[]{:S(2)}) collective-permute-start(f32[2,2560]{1,0:T(2,128)S(1)} %collective-permute-done.1), channel_id=1, source_target_pairs={{0,4},{4,8},{8,12},{12,16},{16,20},{20,24},{24,28},{28,0},{1,5},{5... | collective-permute-start | bytes 61448 | tf_op jit(solution)/shard_map/ppermute | solution.py:50
  139.0 4.1 %collective-permute-start.3 = (f32[2,2560]{1,0:T(2,128)S(1)}, f32[2,2560]{1,0:T(2,128)S(1)}, u32[]{:S(2)}, u32[]{:S(2)}) collective-permute-start(f32[2,2560]{1,0:T(2,128)S(1)} %collective-permute-done.2), channel_id=1, source_target_pairs={{0,4},{4,8},{8,12},{12,16},{16,20},{20,24},{24,28},{28,0},{1,5},{5... | collective-permute-start | bytes 61448 | tf_op jit(solution)/shard_map/ppermute | solution.py:50
  143.1 4.1 %collective-permute-start.4 = (f32[2,2560]{1,0:T(2,128)S(1)}, f32[2,2560]{1,0:T(2,128)S(1)}, u32[]{:S(2)}, u32[]{:S(2)}) collective-permute-start(f32[2,2560]{1,0:T(2,128)S(1)} %collective-permute-done.3), channel_id=1, source_target_pairs={{0,4},{4,8},{8,12},{12,16},{16,20},{20,24},{24,28},{28,0},{1,5},{5... | collective-permute-start | bytes 61448 | tf_op jit(solution)/shard_map/ppermute | solution.py:50
  147.2 4.1 %collective-permute-start.5 = (f32[2,2560]{1,0:T(2,128)S(1)}, f32[2,2560]{1,0:T(2,128)S(1)}, u32[]{:S(2)}, u32[]{:S(2)}) collective-permute-start(f32[2,2560]{1,0:T(2,128)S(1)} %collective-permute-done.4), channel_id=1, source_target_pairs={{0,4},{4,8},{8,12},{12,16},{16,20},{20,24},{24,28},{28,0},{1,5},{5... | collective-permute-start | bytes 61448 | tf_op jit(solution)/shard_map/ppermute | solution.py:50
  151.3 4.1 %collective-permute-start.6 = (f32[2,2560]{1,0:T(2,128)S(1)}, f32[2,2560]{1,0:T(2,128)S(1)}, u32[]{:S(2)}, u32[]{:S(2)}) collective-permute-start(f32[2,2560]{1,0:T(2,128)S(1)} %collective-permute-done.5), channel_id=1, source_target_pairs={{0,4},{4,8},{8,12},{12,16},{16,20},{20,24},{24,28},{28,0},{1,5},{5... | collective-permute-start | bytes 61448 | tf_op jit(solution)/shard_map/ppermute | solution.py:50
  155.9 87.1 %copy-start.9 = (f32[2048]{0:T(1024)S(1)}, f32[2048]{0:T(1024)}, u32[]{:S(2)}) copy-start(f32[2048]{0:T(1024)} %param.22) | copy-start | bytes 24580
  243.1 18.2 %copy-start.2 = (f32[16,2048]{1,0:T(8,128)}, f32[16,2048]{1,0:T(8,128)S(1)}, u32[]{:S(2)}) copy-start(f32[16,2048]{1,0:T(8,128)S(1)} %get-tuple-element.116) | copy-start | bytes 393220
  285.0 0.7 copy-start.4
  285.0 48.1 %copy-start.1 = (f32[4,36]{1,0:T(4,128)S(1)}, f32[4,36]{1,0:T(4,128)}, u32[]{:S(2)}) copy-start(f32[4,36]{1,0:T(4,128)} %param.27) | copy-start | bytes 1732
Sparse Core Ops, SparseCore 0:
  285.8 33.6 reduce-scatter.1
